TPU v7x, 256 devices: a whole 4x4x8 slice. The times are simulated.
256 devices in a mesh: row: 32 (over x, z_hi, core), col: 8 (over z_lo, y).
Axes of the slice: x: 4, y: 4, z: 8 (z_hi: 4, z_lo: 2; z = z_hi * 2 + z_lo), core: 2. Of those that a mesh axis runs over, the one named last changes fastest.
Arguments:
- grad_out: float32 [131072, 128], P(('col', 'row')), may hold values from -6 to 6
- features: float32 [131072, 128], P(('row', 'col')), may hold values from -0.015625 to 0.015625
- weight: float32 [128, 128], replicated, may hold values from -0.5 to 0.5
- adj_values: float32 [8, 1024, 3, 128, 128], P('col', 'row'), may hold values from -0.15625 to 0.15625
- row_block: int32 [8, 1024, 3], P('col', 'row'), may hold values from 0 to 3
- col_block: int32 [8, 1024, 3], P('col', 'row'), may hold values from 0 to 31
- counts: int32 [8, 1024], P('col', 'row'), may hold values from 0 to 3, as said below
Outputs:
- input_grad: float32 [131072, 128], P(('row', 'col'))
- weight_grad: float32 [128, 128], replicated
Inputs may be any that keep to these rules, and one draw needn't show every extreme that they name: counts[c, j] is the number of leading slots of grid cell (c, j) that hold blocks of A; later slots hold values that are not part of A.
All inputs are finite; a program needn't handle non-finite values.
Results may differ from a plain program's by a relative error of at most 0.0003.
Values sent between devices are 32-bit elements; how exact they have to be, the bound alone decides.
A program may use at most 64 MiB of HBM per device.

v0:
```python
import jax
import jax.numpy as jnp
from jax import lax
from jax.sharding import PartitionSpec as P

WIDTH = 128
BLOCK = 128
SLOTS = 3
NODE_DEV = 512
ROW_BLOCKS = 4


def slot_products(part_values, picked):
    return jnp.einsum("ksab,ksaf->ksbf", part_values, picked, precision=lax.Precision.HIGHEST)


def combine(products, part_onehot):
    return jnp.einsum("ksm,ksbf->mbf", part_onehot, products, precision=lax.Precision.HIGHEST)


def local(grad_out, features, weight, adj_values, row_block, col_block, counts):
    sections = lax.axis_size("row")
    col_blocks = lax.axis_size("col") * NODE_DEV // BLOCK
    values = adj_values[0]
    slot_rows = row_block[0]
    slot_cols = col_block[0]
    live_slot = (jnp.arange(SLOTS, dtype=jnp.int32)[None, :] < counts[0][:, None]).astype(
        jnp.float32
    )
    onehot = (
        slot_cols[..., None] == jnp.arange(col_blocks, dtype=jnp.int32)[None, None, :]
    ).astype(jnp.float32) * live_slot[..., None]
    gathered = lax.all_gather(grad_out, "row", axis=0, tiled=True)
    blocks = gathered.reshape(sections * ROW_BLOCKS, BLOCK, WIDTH)
    block_index = jnp.arange(sections, dtype=jnp.int32)[:, None] * ROW_BLOCKS + slot_rows
    products = slot_products(values, blocks[block_index])
    partial_value = None
    partial_value = combine(products, onehot).reshape(col_blocks * BLOCK, WIDTH)
    reduced = lax.psum_scatter(partial_value, "col", scatter_dimension=0, tiled=True)
    input_grad = jnp.dot(
        reduced, weight.T, precision=lax.Precision.HIGHEST, preferred_element_type=jnp.float32
    )
    local_terms = jnp.dot(
        features.T, reduced, precision=lax.Precision.HIGHEST, preferred_element_type=jnp.float32
    )
    weight_grad = lax.psum(local_terms, ("row", "col"))
    return (input_grad, weight_grad)


def solution(mesh):
    return jax.shard_map(
        local,
        mesh=mesh,
        in_specs=(
            P(("col", "row"), None),
            P(("row", "col"), None),
            P(),
            P("col", "row", None, None, None),
            P("col", "row", None),
            P("col", "row", None),
            P("col", "row"),
        ),
        out_specs=(P(("row", "col"), None), P()),
        check_vma=False,
    )
```

profile of v0, /device:TPU:1, one launch (start us, length us, event | category | flops | bytes accessed | tf_op | source)
XLA Modules:
  0.0 426.1 jit_solution(7761816665117667839)
XLA Ops:
  7.2 0.0 copy-start
  7.2 0.0 all-gather.2.cloned.1.call-start
  7.2 0.7 all-gather.2.cloned.1.call-update
  7.9 0.0 reduce-scatter.2.cloned.1.call-start
  8.0 0.7 compare_select_fusion
  8.7 0.1 copy.11
  8.7 0.1 reshape.85
  8.9 0.7 copy.18
  9.5 0.7 fusion.12
  10.2 80.7 %all-gather.2.cloned.1.call-done = f32[16384,128]{1,0:T(8,128)} async-done(((f32[512,128]{1,0:T(8,128)}), f32[16384,128]{1,0:T(8,128)}) %all-gather.2.cloned.1.call-update) | async-done | bytes 8388624 | tf_op jit(solution)/shard_map/all_gather | solution.py:33
  90.9 7.0 %gather_fusion = f32[96,128,128]{2,1,0:T(8,128)} fusion(f32[128,128,128]{2,1,0:T(8,128)} %bitcast.36, s32[1024]{0:T(1024)S(1)} %pad_clamp_fusion), kind=kCustom, calls=%fused_computation | custom fusion | bytes 12583296 | tf_op jit(solution)/shard_map/gather | solution.py:36
  98.0 14.8 %fusion.2 = f32[32,3,128,128]{3,2,1,0:T(8,128)} fusion(f32[32,3,128,128]{3,2,1,0:T(8,128)} %bitcast.34, f32[1,32,3,128,128]{4,3,2,1,0:T(8,128)} %param.10), kind=kOutput, calls=%fused_computation.3 | convolution fusion | flops 2415919104 | bytes 18874368 | tf_op jit(solution)/shard_map/ksab,ksaf->ksbf/dot_general | solution.py:14
  112.8 6.7 %copy.14 = f32[32,3,128,128]{2,0,1,3:T(8,128)} copy(f32[32,3,128,128]{3,2,1,0:T(8,128)} %fusion.2) | data formatting | bytes 12582912 | tf_op jit(solution)/shard_map/ksab,ksaf->ksbf/dot_general | solution.py:14
  119.4 7.1 %fusion.4 = f32[32,128,128]{2,0,1:T(8,128)S(1)} fusion(f32[32,3,128,128]{2,0,1,3:T(8,128)} %copy.14, f32[32,3]{0,1:T(4,128)S(1)} %fusion.12, s32[32,3]{0,1:T(4,128)S(1)} %bitcast.37), kind=kOutput, calls=%fused_computation.5 | convolution fusion | flops 603985920 | bytes 8389376 | tf_op jit(solution)/shard_map/ksm,ksbf->mbf/dot_general | solution.py:18
  126.5 2.6 copy.12
  129.1 0.0 reduce-scatter.2.cloned.1.call-update
  129.1 0.0 all-reduce.2.cloned.1.call-start
  129.1 40.6 %reduce-scatter.2.cloned.1.call-done = f32[512,128]{1,0:T(8,128)} async-done(((f32[4096,128]{1,0:T(8,128)}), f32[512,128]{1,0:T(8,128)}) %reduce-scatter.2.cloned.1.call-update) | async-done | bytes 262160 | tf_op jit(solution)/shard_map/reduce_scatter | solution.py:39
  169.8 0.0 copy-done
  169.8 2.2 convolution_bitcast_fusion
  171.9 0.0 all-reduce.2.cloned.1.call-update
  172.0 2.0 fusion.14
  174.0 244.0 %all-reduce.2.cloned.1.call-done = f32[128,128]{0,1:T(8,128)} async-done(((f32[128,128]{0,1:T(8,128)}), f32[128,128]{0,1:T(8,128)}) %all-reduce.2.cloned.1.call-update) | async-done | bytes 65552 | tf_op jit(solution)/shard_map/psum | solution.py:46
  418.0 1.6 copy.13
  (4 shorter events, 0.0 us)
Async XLA Ops:
  7.2 162.6 %copy-start = (f32[512,128]{1,0:T(8,128)S(1)}, f32[512,128]{1,0:T(8,128)}, u32[]{:S(2)}) copy-start(f32[512,128]{1,0:T(8,128)} %param.8) | copy-start | bytes 786436
  7.2 83.7 %all-gather.2.cloned.1.call-start = ((), (), s32[]{:S(2)}) async-start(), calls=%async_computation.1 | async-start | bytes 8650752 | tf_op jit(solution)/shard_map/all_gather | solution.py:33
  7.9 161.9 %reduce-scatter.2.cloned.1.call-start = ((), (), s32[]{:S(2)}) async-start(), calls=%async_computation.2 | async-start | bytes 2359296 | tf_op jit(solution)/shard_map/reduce_scatter | solution.py:39
  119.4 52.5 %copy-start.1 = (f32[128,128]{1,0:T(8,128)S(1)}, f32[128,128]{1,0:T(8,128)}, u32[]{:S(2)}) copy-start(f32[128,128]{1,0:T(8,128)} %param.9) | copy-start | bytes 196612
  129.1 288.9 %all-reduce.2.cloned.1.call-start = ((), (), s32[]{:S(2)}) async-start(), calls=%async_computation.3 | async-start | bytes 131072 | tf_op jit(solution)/shard_map/psum | solution.py:46
Sparse Core Ops, SparseCore 0:
  10.6 80.3 all-gather.1
  129.2 40.5 reduce-scatter.1
  175.9 242.1 all-reduce.1
where the time goes:
time: 426 us
  waiting for transfers between devices  366 us (86%)
  matrix products  26.1 us (6%)
  local copies, waits for them, and re-layouts  18.7 us (4%)
  between operations  13.8 us (3%)
    psum x1, waiting for transfers between devices, local(): weight_grad = lax.psum(local_terms, ('row', 'col'))  244 us
    all_gather x1, waiting for transfers between devices, local(): gathered = lax.all_gather(grad_out, 'row', axis=0, tiled=True)  80.7 us
    reduce_scatter x1, waiting for transfers between devices, local(): lax.psum_scatter(partial_value, 'col', scatter_dimension=0, tiled=True)  40.6 us
    dot_general x1, matrix products, slot_products(): jnp.einsum('ksab,ksaf->ksbf', part_values, picked, precision=lax.Precisio...  14.8 us
  transfers between devices with their start and end apart: 3, of which 3 were waited for; matrix products, arithmetic and copies ran while one was open for 1% of the time, Pallas kernels for 0%

commit v1 on v0

v1 whole, which is shorter than its diff:
```python
import functools

import jax
import jax.numpy as jnp
from jax import lax
from jax.experimental import pallas as pl
from jax.experimental.pallas import tpu as pltpu
from jax.sharding import PartitionSpec as P

WIDTH = 128
BLOCK = 128
SLOTS = 3
SECTIONS = 32
CELLS = SECTIONS * SLOTS
COL_BLOCKS = 32
CHUNKS = (32, 32, 32, 32)
BATCHES = ((0, 1, 2), (3,))
STAGES = {
    "T0": 0.0, "T1": 0.35, "T2": 0.75, "T3": 1.8, "T4": 2.4, "T5": 2.8,
    "C0": 2.81, "C1": 2.9, "C2": 3.1, "C3": 3.3,
    "R0": 3.32, "R1": 3.6, "R2": 3.9, "R3": 4.2,
}
MESH = pl.DeviceIdType.MESH
HIGHEST = lax.Precision.HIGHEST


def split(v):
    high = v.astype(jnp.bfloat16)
    return high, (v - high.astype(jnp.float32)).astype(jnp.bfloat16)


def starts():
    total, at = 0, []
    for f in CHUNKS:
        at.append(total)
        total += f
    return at


def kernel(
    meta, grad_hbm, feats_hbm, weight_hbm, adj_hbm, ig_out, wg_out,
    adj, halves, grad, feats, weight, run, csum, wgt, local_sem, send_sem, recv_sem, *bufs,
):
    n = len(CHUNKS)
    per = 8
    chunk_bufs = [bufs[per * j : per * (j + 1)] for j in range(n)]
    sum_bufs = [bufs[per * n + 3 * b : per * n + 3 * b + 3] for b in range(len(BATCHES))]
    at = starts()

    row, col = lax.axis_index("row"), lax.axis_index("col")
    x, zh, h = row // 8, (row // 2) % 4, row % 2
    zl, y = col // 4, col % 4
    corner = x * 2 + h

    def place(x_, zh_, h_):
        return {"row": x_ * 8 + zh_ * 2 + h_, "col": col}

    def place_col(zl_, y_):
        return {"row": row, "col": zl_ * 4 + y_}

    xp, xm, xo = (x + 1) % 4, (x + 3) % 4, (x + 2) % 4
    zp, zm, zo = (zh + 1) % 4, (zh + 3) % 4, (zh + 2) % 4
    yp, ym, yo = (y + 1) % 4, (y + 3) % 4, (y + 2) % 4
    sib = place(x, zh, 1 - h)
    to_xp, to_xm = place(xp, zh, h), place(xm, zh, h)
    to_zp, to_zm = place(x, zp, h), place(x, zm, h)
    to_yp, to_ym = place_col(zl, yp), place_col(zl, ym)
    to_zl = place_col(1 - zl, y)
    col_peers = [{"row": row, "col": (col + d) % 8} for d in range(1, 8)]
    corner_peers = []
    for d in range(1, 8):
        o = (corner + d) % 8
        corner_peers.append(place(o // 2, zh, o % 2))
    zh_peers = [place(x, (zh + d) % 4, h) for d in range(1, 4)]

    def load(k, src, dst):
        c = pltpu.make_async_copy(src, dst, local_sem.at[k])
        c.start()
        return c

    grad_load = load(0, grad_hbm, grad)
    adj_load = load(1, adj_hbm, adj)
    feats_load = load(2, feats_hbm, feats)
    weight_load = load(3, weight_hbm, weight)

    barrier = pltpu.get_barrier_semaphore()
    for peer in col_peers + corner_peers + zh_peers:
        pl.semaphore_signal(barrier, inc=1, device_id=peer, device_id_type=MESH)

    grad_load.wait()
    hx = h * 4 + x
    for rb in range(4):
        turned = grad[rb * BLOCK : (rb + 1) * BLOCK, :].T
        for j in range(n):
            chunk_bufs[j][0][hx, zh, rb] = turned[at[j] : at[j] + CHUNKS[j], :]

    pl.semaphore_wait(barrier, 17)

    sends = []

    def push(src, dst, peer):
        k = len(sends)
        c = pltpu.make_async_remote_copy(
            src_ref=src, dst_ref=dst, send_sem=send_sem.at[k], recv_sem=recv_sem.at[k],
            device_id=peer, device_id_type=MESH,
        )
        c.start()
        sends.append(c)
        return c

    pending = {}

    def move(ref, peer):
        return push(ref, ref, peer)

    def take(*key):
        for c in pending.pop(key):
            c.wait_recv()

    A, B = pl.ds(0, 3), pl.ds(3, 1)

    def stage_T0(j):
        g = chunk_bufs[j][0]
        pending["T0", j] = [
            move(g.at[hx, zh, A], to_zp), move(g.at[hx, zh, A], to_zm),
            move(g.at[hx, zh, B], to_xp), move(g.at[hx, zh, B], to_xm),
        ]

    def lows(j):
        half = CHUNKS[j] // 2
        return pl.ds(0, half), pl.ds(half, half)

    def stage_T1(j):
        g = chunk_bufs[j][0]
        lo, hi = lows(j)
        take("T0", j)
        pending["T1", j] = [
            move(g.at[hx, zm, A, lo], to_zp), move(g.at[hx, zp, A, hi], to_zm),
            move(g.at[h * 4 + xm, zh, B, lo], to_xp), move(g.at[h * 4 + xp, zh, B, hi], to_xm),
        ]

    ours = pl.ds(h * 4, 4)

    def stage_T2(j):
        g = chunk_bufs[j][0]
        take("T1", j)
        pending["T2", j] = [
            move(g.at[hx, :, A], to_xp), move(g.at[hx, :, A], to_xm),
            move(g.at[ours, zh, B], to_zp), move(g.at[ours, zh, B], to_zm),
        ]
        pending["S", j] = [move(g.at[hx, :, A], sib), move(g.at[ours, zh, B], sib)]

    def stage_T3(j):
        g = chunk_bufs[j][0]
        lo, hi = lows(j)
        take("T2", j)
        pending["T3", j] = [
            move(g.at[h * 4 + xm, :, A, lo], to_xp), move(g.at[h * 4 + xp, :, A, hi], to_xm),
            move(g.at[ours, zm, B, lo], to_zp), move(g.at[ours, zp, B, hi], to_zm),
        ]
        pending["S", j] += [
            move(g.at[h * 4 + xm, :, A], sib), move(g.at[h * 4 + xp, :, A], sib),
            move(g.at[ours, zm, B], sib), move(g.at[ours, zp, B], sib),
        ]

    def stage_T4(j):
        g = chunk_bufs[j][0]
        take("T3", j)
        pending["S", j] += [move(g.at[h * 4 + xo, :, A], sib), move(g.at[ours, zo, B], sib)]

    def stage_T5(j):
        take("S", j)

    def stage_C(j, part):
        g, part_sums = chunk_bufs[j][0], chunk_bufs[j][1]
        f = CHUNKS[j]
        size = CELLS // 4
        first = part * size

        def step(p, acc):
            block = halves[meta[0, p]]
            picked = g[meta[1, p], meta[2, p], meta[3, p]]
            high, low = split(picked)
            both = jnp.concatenate([high, low], axis=0)
            r = jnp.dot(both, block, preferred_element_type=jnp.float32)
            product = r[:f, :BLOCK] + (r[f:, :BLOCK] + r[:f, BLOCK:])
            acc = product + jnp.where(meta[4, p] > 0, acc, 0.0)
            run[p, :f] = acc
            return acc

        init = jnp.zeros((f, BLOCK), jnp.float32) if part == 0 else run[first - 1, :f]
        lax.fori_loop(first, first + size, step, init, unroll=4)
        if part == 3:
            def collect(m, carry):
                v = run[meta[5, m], :f]
                part_sums[m // 16, (m // 4) % 4, m % 4] = jnp.where(meta[6, m] > 0, v, 0.0)
                return carry

            lax.fori_loop(0, COL_BLOCKS, collect, 0, unroll=4)

    def stage_R0(j):
        p, r1p, r1m = chunk_bufs[j][1:4]
        pending["R0", j] = [
            push(p.at[:, yo, pl.ds(0, 2)], r1p, to_yp),
            push(p.at[:, yo, pl.ds(2, 2)], r1m, to_ym),
        ]

    def stage_R1(j):
        p, r1p, r1m, r2p, r2m = chunk_bufs[j][1:6]
        take("R0", j)
        for z in range(2):
            p[z, yp, 0:2] = p[z, yp, 0:2] + r1p[z]
            p[z, ym, 2:4] = p[z, ym, 2:4] + r1m[z]
        pending["R1", j] = [push(p.at[:, yp], r2p, to_yp), push(p.at[:, ym], r2m, to_ym)]

    def stage_R2(j):
        p, r1p, r1m, r2p, r2m, s, r3 = chunk_bufs[j][1:8]
        take("R1", j)
        for z in range(2):
            s[z] = p[z, y] + (r2p[z] + r2m[z])
        pending["R2", j] = [push(s.at[1 - zl], r3, to_zl)]

    def stage_R3(j):
        s, r3 = chunk_bufs[j][6:8]
        take("R2", j)
        f = CHUNKS[j]
        total = jnp.zeros((f, WIDTH), jnp.float32)
        for b in range(4):
            v = s[zl, b] + r3[b]
            csum[b, at[j] : at[j] + f, :] = v
            total += jnp.dot(
                v, feats[b * BLOCK : (b + 1) * BLOCK, :], precision=HIGHEST,
                preferred_element_type=jnp.float32,
            )
        wgt[at[j] : at[j] + f, :] = total

    def window(b):
        first = at[BATCHES[b][0]]
        return pl.ds(first, sum(CHUNKS[j] for j in BATCHES[b]))

    def fold(buf, count):
        total = buf[0]
        for i in range(1, count):
            total += buf[i]
        return total

    def stage_W0(b):
        buf = sum_bufs[b][0]
        buf[col] = wgt[window(b), :]
        pending["W0", b] = [push(buf.at[col], buf.at[col], peer) for peer in col_peers]

    def stage_W1(b):
        take("W0", b)
        buf = sum_bufs[b][1]
        buf[corner] = fold(sum_bufs[b][0], 8)
        pending["W1", b] = [push(buf.at[corner], buf.at[corner], peer) for peer in corner_peers]

    def stage_W2(b):
        take("W1", b)
        buf = sum_bufs[b][2]
        buf[zh] = fold(sum_bufs[b][1], 8)
        pending["W2", b] = [push(buf.at[zh], buf.at[zh], peer) for peer in zh_peers]

    def stage_W3(b):
        take("W2", b)
        wgt[window(b), :] = fold(sum_bufs[b][2], 4)

    unit = CHUNKS[0]
    plan = []
    for j in range(n):
        begin = at[j] / unit
        for name, offset in STAGES.items():
            plan.append((begin + offset, len(plan), name, j))
    for b, batch in enumerate(BATCHES):
        begin = at[batch[-1]] / unit + STAGES["R3"]
        for i in range(4):
            plan.append((begin + 0.01 + 0.3 * i, len(plan), "W" + str(i), b))
    plan.sort()

    split_parts = 4
    done_split = 0

    def split_part(i):
        if i == 0:
            adj_load.wait()
        size = CELLS // split_parts

        def body(s, carry):
            high, low = split(adj[s])
            halves[s, :, :BLOCK] = high
            halves[s, :, BLOCK:] = low
            return carry

        lax.fori_loop(i * size, (i + 1) * size, body, 0, unroll=2)

    for _, _, name, j in plan:
        if name == "R3" and j == 0:
            feats_load.wait()
            weight_load.wait()
        if name == "W1" and j == len(BATCHES) - 1:
            turned_weight = weight[...].T
            for b in range(4):
                ig_out[b * BLOCK : (b + 1) * BLOCK, :] = jnp.dot(
                    csum[b].T, turned_weight, precision=HIGHEST, preferred_element_type=jnp.float32
                )
        if name[0] == "C":
            stage_C(j, int(name[1]))
        elif name[0] == "T":
            (stage_T0, stage_T1, stage_T2, stage_T3, stage_T4, stage_T5)[int(name[1])](j)
            if done_split < split_parts:
                split_part(done_split)
                done_split += 1
        elif name[0] == "R":
            (stage_R0, stage_R1, stage_R2, stage_R3)[int(name[1])](j)
        else:
            (stage_W0, stage_W1, stage_W2, stage_W3)[int(name[1])](j)

    wg_out[...] = wgt[...].T
    for c in sends:
        c.wait_send()


def scratch():
    f32 = jnp.float32
    out = [
        pltpu.VMEM((CELLS, BLOCK, BLOCK), f32),
        pltpu.VMEM((CELLS, BLOCK, 2 * BLOCK), jnp.bfloat16),
        pltpu.VMEM((512, WIDTH), f32),
        pltpu.VMEM((512, WIDTH), f32),
        pltpu.VMEM((WIDTH, WIDTH), f32),
        pltpu.VMEM((CELLS, max(CHUNKS), BLOCK), f32),
        pltpu.VMEM((4, WIDTH, BLOCK), f32),
        pltpu.VMEM((WIDTH, WIDTH), f32),
        pltpu.SemaphoreType.DMA((4,)),
    ]
    count = 29 * len(CHUNKS) + 17 * len(BATCHES)
    out += [pltpu.SemaphoreType.DMA((count,)), pltpu.SemaphoreType.DMA((count,))]
    for f in CHUNKS:
        for lead in ((8, 4, 4), (2, 4, 4), (2, 2), (2, 2), (2, 4), (2, 4), (2, 4), (4,)):
            out.append(pltpu.VMEM(lead + (f, BLOCK), f32))
    for batch in BATCHES:
        f = sum(CHUNKS[j] for j in batch)
        for lead in (8, 8, 4):
            out.append(pltpu.VMEM((lead, f, WIDTH), f32))
    return out


def prepare(row_block, col_block, counts):
    index = jnp.arange(CELLS, dtype=jnp.int32)
    k = index // SLOTS
    live = (jnp.arange(SLOTS, dtype=jnp.int32)[None, :] < counts[:, None]).reshape(CELLS)
    blocks = jnp.where(live, col_block.reshape(CELLS), COL_BLOCKS)
    keys = blocks * 128 + index
    rank = jnp.sum((keys[None, :] < keys[:, None]).astype(jnp.int32), axis=1)
    place = jnp.arange(128, dtype=jnp.int32)
    hit = rank[:, None] == place[None, :]
    fields = jnp.stack(
        [index, (k % 2) * 4 + k // 8, (k // 2) % 4, row_block.reshape(CELLS), blocks]
    )
    ordered = jnp.sum(jnp.where(hit[None], fields[:, :, None], 0), axis=1)
    same = jnp.concatenate(
        [jnp.zeros((1,), jnp.int32), (ordered[4, 1:] == ordered[4, :-1]).astype(jnp.int32)]
    )
    upto = jnp.sum((blocks[:, None] <= place[None, :]).astype(jnp.int32), axis=0)
    present = jnp.any(blocks[:, None] == place[None, :], axis=0).astype(jnp.int32)
    last = jnp.maximum(upto - 1, 0)
    return jnp.concatenate([ordered[:4], same[None], last[None], present[None]], axis=0)


def local(grad_out, features, weight, adj_values, row_block, col_block, counts):
    meta = prepare(row_block[0], col_block[0], counts[0])
    anyspace = pl.BlockSpec(memory_space=pl.ANY)
    return pl.pallas_call(
        kernel,
        out_shape=(
            jax.ShapeDtypeStruct((512, WIDTH), jnp.float32),
            jax.ShapeDtypeStruct((WIDTH, WIDTH), jnp.float32),
        ),
        in_specs=[pl.BlockSpec(memory_space=pltpu.SMEM)] + [anyspace] * 4,
        out_specs=(pl.BlockSpec(memory_space=pltpu.VMEM),) * 2,
        scratch_shapes=scratch(),
        compiler_params=pltpu.CompilerParams(
            collective_id=0, has_side_effects=True, vmem_limit_bytes=52 * 1024 * 1024
        ),
        cost_estimate=pl.CostEstimate(
            flops=1_200_000_000, bytes_accessed=7_000_000, transcendentals=0
        ),
    )(meta, grad_out, features, weight, adj_values.reshape(CELLS, BLOCK, BLOCK))


def solution(mesh):
    return jax.shard_map(
        local,
        mesh=mesh,
        in_specs=(
            P(("col", "row"), None),
            P(("row", "col"), None),
            P(),
            P("col", "row", None, None, None),
            P("col", "row", None),
            P("col", "row", None),
            P("col", "row"),
        ),
        out_specs=(P(("row", "col"), None), P()),
        check_vma=False,
    )
```

time: 426 us -> 135 us (0.32)
  waiting for transfers between devices: 366 us -> 0 us
  Pallas kernels: 0 us -> 126 us
  matrix products: 26.1 us -> 0 us
  between operations: 13.8 us -> 0.71 us
  local copies, waits for them, and re-layouts: 18.7 us -> 6.17 us
    psum x1 -> x0, waiting for transfers between devices: 244 us -> none  [local(): weight_grad = lax.psum(local_terms, ('row', 'col'))]
    pallas_call x0 -> x1, Pallas kernels: none -> 126 us  [local(): pl.pallas_call(kernel, out_shape=(jax.ShapeDtypeStruct((512, WIDTH), jnp....]
    all_gather x1 -> x0, waiting for transfers between devices: 80.7 us -> none  [local(): gathered = lax.all_gather(grad_out, 'row', axis=0, tiled=True)]
    reduce_scatter x1 -> x0, waiting for transfers between devices: 40.6 us -> none  [local(): lax.psum_scatter(partial_value, 'col', scatter_dimension=0, tiled=True)]
    dot_general x4 -> x0, matrix products: 26.1 us -> none  [the longest x1 14.8 us: slot_products(): jnp.einsum('ksab,ksaf->ksbf', part_values, picked, precision=lax.Precisio...]
    dot_general x2 -> x0, local copies, waits for them, and re-layouts: 9.22 us -> none  [the longest x1 6.67 us: slot_products(): jnp.einsum('ksab,ksaf->ksbf', part_values, picked, precision=lax.Precisio...]
    gather x1 -> x0, local copies, waits for them, and re-layouts: 7.03 us -> none  [local(): products = slot_products(values, blocks[block_index])]
  transfers between devices with their start and end apart: 3 -> 0, of which waited for: 3 -> 0; matrix products, arithmetic and copies ran while one was open for 1% -> 0% of each run, Pallas kernels for 0% -> 0%
where the time goes in v1:
time: 135 us; the launch traced here: 134 us
  Pallas kernels  126 us (93%)
  local copies, waits for them, and re-layouts  6.17 us (5%)
  other arithmetic  1.54 us (1%)
    pallas_call x1, Pallas kernels, local(): pl.pallas_call(kernel, out_shape=(jax.ShapeDtypeStruct((512, WIDTH), jnp....  126 us
    unnamed x10, local copies, waits for them, and re-layouts  5.6 us

profile of v1, /device:TPU:1, one launch (start us, length us, event | category | flops | bytes accessed | tf_op | source)
XLA Modules:
  0.0 134.4 jit_solution(5497281110083798631)
XLA Ops:
  0.7 0.7 iota_compare_fusion.3
  1.4 0.1 lt.72
  1.5 0.1 lt.66
  1.6 0.8 copy.15
  2.4 0.1 reshape_squeeze.6
  2.5 0.1 reshape_squeeze.5
  2.6 0.2 convert_reduce_fusion.1
  2.8 0.1 convert_reduce_fusion
  2.9 0.1 fusion
  3.0 0.1 iota_compare_fusion.2
  3.1 0.8 copy.16
  3.9 0.1 stack_reshape_squeeze.3
  4.0 0.1 select_reduce_fusion
  4.2 0.1 compare_bitcast_fusion
  4.2 0.1 fusion.3
  4.3 0.0 copy-start
  4.3 0.9 copy-done
  5.3 0.0 copy-start.1
  5.3 0.9 copy-done.1
  6.2 0.0 copy-start.2
  6.2 0.8 copy-done.2
  7.1 126.0 %shard_map.86 = (f32[512,128]{1,0:T(8,128)S(1)}, f32[128,128]{1,0:T(8,128)S(1)}) custom-call(s32[7,128]{1,0:T(8,128)S(1)} %pad_add_fusion.meta, f32[512,128]{1,0:T(8,128)S(1)} %copy-done, f32[512,128]{1,0:T(8,128)S(1)} %copy-done.1, f32[128,128]{1,0:T(8,128)S(1)} %copy-done.2, f32[96,128,128]{2,1,0:T(8,128)} %bitcast.10), custom_call_target="tpu_custom_call" | custom-call | flops 1200000000 | bytes 7000000 | tf_op jit(solution)/shard_map/pallas_call | solution.py:373
  133.0 0.7 copy.20
  133.7 0.6 copy.21
  (9 shorter events, 0.1 us)
Async XLA Ops:
  4.3 1.0 copy-start
  5.3 0.9 copy-start.1
  6.2 0.8 copy-start.2

commit v2 on v0

v2 whole, which is shorter than its diff:
```python
import jax
import jax.numpy as jnp
from jax import lax
from jax.experimental import pallas as pl
from jax.experimental.pallas import tpu as pltpu
from jax.sharding import PartitionSpec as P

WIDTH = 128
BLOCK = 128
SLOTS = 3
SECTIONS = 32
CELLS = SECTIONS * SLOTS
GROUPS = ((0, 24), (24, 48), (72, 24))
PARTS = ((0, 0, 24), (1, 24, 24), (1, 48, 24), (2, 72, 24))
COL_BLOCKS = 32
NODE_DEV = 512
CHUNKS = (16, 32, 32, 32, 16)
ACROSS = (1, 1, 1, 0, 0)
STRAIGHT = (0, 0, 0, 0, 1)
EARLY = 4
ORDER = (
    ("U0", 0), ("U0", 1), ("U0", 2), ("U1", 0), ("U1", 1), ("U1", 2), ("U2", 0), ("C0", 0), ("U0", 3), ("U2", 1),
    ("C0", 1), ("U2", 2), ("U3", 0), ("C0", 2), ("U0", 4), ("C1", 0), ("C2", 0), ("U1", 3), ("U3", 1), ("U3", 2),
    ("U4", 0), ("C1", 1), ("C2", 1), ("U1", 4), ("C1", 2), ("C3", 0), ("R0", 0), ("U2", 3), ("U4", 1), ("C2", 2),
    ("U4", 2), ("C0", 3), ("C3", 1), ("U2", 4), ("R0", 1), ("C3", 2), ("R0", 2), ("C0", 4), ("U3", 3), ("R1", 0),
    ("U3", 4), ("C1", 3), ("C2", 3), ("U4", 3), ("C1", 4), ("R2", 0), ("U4", 4), ("C2", 4), ("C3", 3), ("R0", 3),
    ("C3", 4), ("R0", 4), ("R1", 1), ("R1", 2), ("R2", 1), ("R2", 2), ("R1", 3), ("R2", 4), ("W0", 0), ("R2", 3),
    ("V0", 0), ("O0", 0), ("W1", 0), ("V1", 0), ("W2", 0), ("V2", 0), ("V3", 0),
)
MESH = pl.DeviceIdType.MESH
HIGHEST = lax.Precision.HIGHEST


def starts():
    total, at = 0, []
    for f in CHUNKS:
        at.append(total)
        total += f
    return at


def split(v):
    high = v.astype(jnp.bfloat16).astype(jnp.float32)
    return high, v - high


def order_slots(rowb, colb, counts, x, zh, h, zl, y):
    lanes = lax.broadcasted_iota(jnp.int32, (1, BLOCK), 1)
    k, s = lanes & 31, lanes >> 5
    spare = jnp.zeros((1, SECTIONS), jnp.int32)

    def flat(ref):
        return jnp.concatenate([ref[0:1, :], ref[1:2, :], ref[2:3, :], spare], axis=1)

    rb, cb = flat(rowb), flat(colb)
    live = s < jnp.concatenate([counts[0:1, :]] * 4, axis=1)
    dx = ((k >> 3) - x + 4) & 3
    group = jnp.where(s == SLOTS, 3, jnp.where(dx == 0, 0, jnp.where(dx == 2, 2, 1)))
    key = ((group * 64 + jnp.where(live, cb, COL_BLOCKS)) * 128 + lanes) * 4 + rb
    across = jnp.broadcast_to(key, (BLOCK, BLOCK))
    down = across.T
    rank = jnp.sum((across < down).astype(jnp.int32), axis=1, keepdims=True)
    spot = lax.broadcasted_iota(jnp.int32, (BLOCK, BLOCK), 1)
    okey = jnp.sum(jnp.where(rank == spot, down, 0), axis=0, keepdims=True)
    oi = (okey >> 2) & 127
    ok, block = oi & 31, (okey >> 9) & 63
    odx, odz = ((ok >> 3) - x + 4) & 3, (((ok >> 1) & 3) - zh + 4) & 3
    before = pltpu.roll(block, 1, 1)
    first = (lanes == 0) | (lanes == GROUPS[1][0]) | (lanes == GROUPS[2][0])
    keep = jnp.where((block == before) & jnp.logical_not(first), 1, 0)
    zpos = jnp.where(odz == 0, 2, jnp.where(odz == 1, 0, jnp.where(odz == 2, 3, 1)))
    rows = [
        ok * SLOTS + (oi >> 5), jnp.where(odx == 3, 1, 0), (ok + h) & 1, zpos, okey & 3, keep,
    ]
    owner, column = down >> 15, (down >> 9) & 63
    wanted = (((spot >> 4) + zl) & 1) * 16 + (((spot >> 2) + y) & 3) * 4 + (spot & 3)
    for g, (begin, _) in enumerate(GROUPS):
        ours = owner == g
        upto = jnp.sum((ours & (column <= wanted)).astype(jnp.int32), axis=0, keepdims=True)
        here = jnp.sum((ours & (column == wanted)).astype(jnp.int32), axis=0, keepdims=True)
        rows.append(jnp.where(here > 0, begin + upto - 1, CELLS))
    return rows


def kernel(
    rowb, colb, counts, grad_hbm, feats_hbm, weight_hbm, adj_hbm, ig_out, wg_out,
    adj, halves, grad, feats, weight, csum, ig, wg, wgt, wgl, wgf, ordered, meta,
    tiles, crossed, late0, late1, local_sem, send_sem, recv_sem, *bufs,
):
    n = len(CHUNKS)
    at = starts()
    chunk_bufs = [bufs[8 * j : 8 * (j + 1)] for j in range(n)]

    row, col = lax.axis_index("row"), lax.axis_index("col")
    x, zh, h = row // 8, (row // 2) % 4, row % 2
    zl, y = col // 4, col % 4
    deck = zh * 4 + zl * 2 + h
    pillar = x * 4 + y

    def chip(dx, dz):
        return {"row": ((x + dx) % 4) * 8 + ((zh + dz) % 4) * 2 + h, "col": col}

    def on_pillar(d):
        o = (pillar + d) % 16
        return {"row": (o // 4) * 8 + zh * 2 + h, "col": zl * 4 + o % 4}

    def on_deck(d):
        o = (deck + d) % 16
        return {"row": x * 8 + (o // 4) * 2 + o % 2, "col": ((o // 2) % 2) * 4 + y}

    def in_col(dzl, dy):
        return {"row": row, "col": ((zl + dzl) % 2) * 4 + (y + dy) % 4}

    sib = {"row": x * 8 + zh * 2 + 1 - h, "col": col}
    xp, xm, zp, zm = chip(1, 0), chip(3, 0), chip(0, 1), chip(0, 3)
    pillar_peers = [on_pillar(d) for d in range(1, 16)]
    deck_peers = [on_deck(d) for d in range(1, 16)]
    col_steps = [(a, b) for a in range(2) for b in range(4) if (a, b) != (0, 0)]
    col_peers = {step: in_col(*step) for step in col_steps}

    def load(k, src, dst):
        c = pltpu.make_async_copy(src, dst, local_sem.at[k])
        c.start()
        return c

    grad_load = load(0, grad_hbm, grad)
    adj_load = load(1, adj_hbm, adj)
    feats_load = load(2, feats_hbm, feats)
    weight_load = load(3, weight_hbm, weight)

    barrier = pltpu.get_barrier_semaphore()
    greeted = pillar_peers + deck_peers + [col_peers[1, d] for d in range(1, 4)]
    for peer in greeted:
        pl.semaphore_signal(barrier, inc=1, device_id=peer, device_id_type=MESH)

    grad_load.wait()
    for rb in range(4):
        turned = grad[rb * BLOCK : (rb + 1) * BLOCK, :].T
        for j in range(n):
            chunk_bufs[j][0][0, 0, 2, rb] = turned[at[j] : at[j] + CHUNKS[j], :]
    pl.semaphore_wait(barrier, len(greeted))

    sends = []
    pending = {}

    def push(key, src, dst, peer):
        k = len(sends)
        c = pltpu.make_async_remote_copy(
            src_ref=src, dst_ref=dst, send_sem=send_sem.at[k], recv_sem=recv_sem.at[k],
            device_id=peer, device_id_type=MESH,
        )
        c.start()
        sends.append(c)
        pending.setdefault(key, []).append(c)

    def take(*key):
        for c in pending.pop(key):
            c.wait_recv()

    def stage_U(j, d):
        near, mid, far = chunk_bufs[j][:3]
        f, cross = CHUNKS[j], ACROSS[j]
        down, over = pl.ds(0, 4 - cross), pl.ds(4 - cross, cross)
        every = pl.ds(0, 4)

        def half(blocks, i):
            if cross:
                return blocks, pl.ds(i * (f // 2), f // 2)
            return (pl.ds(2 * i, 2),)

        def go(key, src, dst, peer, *index):
            push((key, j), src.at[index], dst.at[index], peer)

        own, plus, minus, both, opposite = 2, 0, 1, pl.ds(0, 2), 3
        if d == 0:
            unit = near.at[0, 0, own]
            go("X0", unit, mid.at[1, 0, own], xp, every)
            go("X0", unit, mid.at[0, 0, own], xm, every)
            go("Z0", unit, near.at[0, 0, minus], zp, every)
            go("Z0", unit, near.at[0, 0, plus], zm, every)
        elif d == 1:
            take("X0", j)
            go("1", mid.at[1, 0, own], far.at[0, 0, own], xp, *half(every, 0))
            go("1", mid.at[0, 0, own], far.at[0, 0, own], xm, *half(every, 1))
            if cross:
                pair = mid.at[:, 0, own, over]
                push(("1", j), pair, mid.at[:, 0, minus, over], zp)
                push(("1", j), pair, mid.at[:, 0, plus, over], zm)
            take("Z0", j)
            go("1", near.at[0, 0, minus], near.at[0, 0, opposite], zp, *half(every, 0))
            go("1", near.at[0, 0, plus], near.at[0, 0, opposite], zm, *half(every, 1))
            pair = near.at[0, 0, both, down]
            push(("1", j), pair, mid.at[1, 0, both, down], xp)
            push(("1", j), pair, mid.at[0, 0, both, down], xm)
        elif d == 2:
            take("1", j)
            push(("2", j), near.at[0, 0, opposite, down], mid.at[1, 0, opposite, down], xp)
            push(("2", j), near.at[0, 0, opposite, down], mid.at[0, 0, opposite, down], xm)
            go("2", mid.at[1, 0], far.at[0, 0], xp, both, *half(down, 0))
            go("2", mid.at[0, 0], far.at[0, 0], xm, both, *half(down, 1))
            if cross:
                push(("2", j), far.at[0, 0, own, over], far.at[0, 0, minus, over], zp)
                push(("2", j), far.at[0, 0, own, over], far.at[0, 0, plus, over], zm)
                lo, hi = half(over, 0), half(over, 1)
                push(("2", j), mid.at[:, 0, minus, *lo], mid.at[:, 0, opposite, *lo], zp)
                push(("2", j), mid.at[:, 0, plus, *hi], mid.at[:, 0, opposite, *hi], zm)
            push(("S", j, 0), near.at[:, 0], near.at[:, 1], sib)
        elif d == 3:
            take("2", j)
            go("3", mid.at[1, 0, opposite], far.at[0, 0, opposite], xp, *half(down, 0))
            go("3", mid.at[0, 0, opposite], far.at[0, 0, opposite], xm, *half(down, 1))
            if cross:
                go("3", far.at[0, 0, minus], far.at[0, 0, opposite], zp, *half(over, 0))
                go("3", far.at[0, 0, plus], far.at[0, 0, opposite], zm, *half(over, 1))
            push(("S", j, 1), mid.at[:, 0], mid.at[:, 1], sib)
        else:
            take("3", j)
            push(("S", j, 2), far.at[:, 0], far.at[:, 1], sib)

    def stage_C(j, part):
        group, begin, size = PARTS[part]
        g, run, f = chunk_bufs[j][group], chunk_bufs[j][7], CHUNKS[j]
        if begin == GROUPS[group][0]:
            take("S", j, group)
            init = jnp.zeros((f, BLOCK), jnp.float32)
        else:
            init = run[begin - 1]

        def step(p, acc):
            block = halves[meta[0, p]]
            high, low = split(g[meta[1, p] if group == 1 else 0, meta[2, p], meta[3, p], meta[4, p]])
            both = jnp.concatenate([high, low], axis=0).astype(jnp.bfloat16)
            r = jnp.dot(both, block, preferred_element_type=jnp.float32)
            product = r[:f, :BLOCK] + (r[f:, :BLOCK] + r[:f, BLOCK:])
            acc = product + jnp.where(meta[5, p] > 0, acc, 0.0)
            run[p] = acc
            return acc

        lax.fori_loop(begin, begin + size, step, init, unroll=4)

    def collect(j):
        part_sums, run = chunk_bufs[j][3], chunk_bufs[j][7]
        run[CELLS] = jnp.zeros((CHUNKS[j], BLOCK), jnp.float32)

        def body(m, carry):
            v = [run[meta[6 + g, m]] for g in range(3)]
            part_sums[m // 16, (m // 4) % 4, m % 4] = (v[0] + v[1]) + v[2]
            return carry

        lax.fori_loop(0, COL_BLOCKS, body, 0, unroll=4)

    def stage_R0(j):
        collect(j)
        p, landing = chunk_bufs[j][3:5]
        if STRAIGHT[j]:
            for i, (a, b) in enumerate(col_steps):
                push(("R0", j), p.at[a, b], landing.at[i], col_peers[a, b])
        else:
            for d in range(1, 4):
                push(("R0", j), p.at[:, d], landing.at[d - 1], col_peers[0, d])

    def stage_R1(j):
        p, landing, s, second = chunk_bufs[j][3:7]
        take("R0", j)
        for z in range(2):
            s[z] = (p[z, 0] + landing[0, z]) + (landing[1, z] + landing[2, z])
        push(("R1", j), s.at[1], second, col_peers[1, 0])

    def stage_R2(j):
        p, landing, s, second = chunk_bufs[j][3:7]
        f = CHUNKS[j]
        take("R0" if STRAIGHT[j] else "R1", j)
        total = jnp.zeros((f, WIDTH), jnp.float32)
        for b in range(4):
            if STRAIGHT[j]:
                v = p[0, 0, b]
                for i in range(7):
                    v += landing[i, b]
            else:
                v = s[0, b] + second[b]
            csum[b, at[j] : at[j] + f, :] = v
            total += jnp.dot(
                v, feats[b * BLOCK : (b + 1) * BLOCK, :], precision=HIGHEST,
                preferred_element_type=jnp.float32,
            )
        if j < EARLY:
            wgt[at[j] : at[j] + f, :] = total
        else:
            wgl[at[j] - at[EARLY] : at[j] - at[EARLY] + f, :] = total

    def fold(buf):
        total = buf[0]
        for i in range(1, 16):
            total += buf[i]
        return total

    def tile(ref, i):
        return ref.at[pl.ds(pl.multiple_of(i * 8, 8), 8)]

    def stage_V(i):
        if i == 0:
            wgt[at[EARLY] :, :] = jnp.zeros((WIDTH - at[EARLY], WIDTH), jnp.float32)
            for d in range(1, 16):
                to = (pillar + d) % 16
                push(("V0",), tile(wgt, to), tiles.at[pillar], pillar_peers[d - 1])
            tiles[pillar] = wgt[pl.ds(pl.multiple_of(pillar * 8, 8), 8), :]
        elif i == 1:
            take("V0")
            crossed[deck] = fold(tiles)
            for d in range(1, 16):
                push(("V1",), crossed.at[deck], crossed.at[deck], deck_peers[d - 1])
        elif i == 2:
            take("V1")
            wgf[pl.ds(pl.multiple_of(pillar * 8, 8), 8), :] = fold(crossed)
            for d in range(1, 16):
                push(("V2",), tile(wgf, pillar), tile(wgf, pillar), pillar_peers[d - 1])
        else:
            take("V2")

    def stage_W(i):
        if i == 0:
            late0[pillar] = wgl[...]
            for d in range(1, 16):
                push(("W0",), late0.at[pillar], late0.at[pillar], pillar_peers[d - 1])
        elif i == 1:
            take("W0")
            late1[deck] = fold(late0)
            for d in range(1, 16):
                push(("W1",), late1.at[deck], late1.at[deck], deck_peers[d - 1])
        else:
            take("W1")

    parts, state = 8, {"done": 0, "sent": 0, "feats": False}

    def prepare():
        i = state["done"]
        state["done"] += 1
        if i == 0:
            ordered[...] = jnp.zeros((16, BLOCK), jnp.int32)
            for r, v in enumerate(order_slots(rowb, colb, counts, x, zh, h, zl, y)):
                ordered[r : r + 1, :] = v
            state["meta"] = load(4, ordered, meta)
            return
        if i == 1:
            adj_load.wait()
            state["meta"].wait()
        if i <= parts:
            size = CELLS // parts

            def body(s, carry):
                high, low = split(adj[s])
                halves[s, :, :BLOCK] = high.astype(jnp.bfloat16)
                halves[s, :, BLOCK:] = low.astype(jnp.bfloat16)
                return carry

            lax.fori_loop((i - 1) * size, i * size, body, 0, unroll=2)

    def drain(upto):
        while state["sent"] < upto:
            sends[state["sent"]].wait_send()
            state["sent"] += 1

    for name, j in ORDER:
        kind, i = name[0], int(name[1])
        if kind == "C":
            while state["done"] <= parts:
                prepare()
        if kind == "U":
            stage_U(j, i)
            prepare()
        elif kind == "C":
            stage_C(j, i)
        elif kind == "R":
            if name == "R2" and not state["feats"]:
                state["feats"] = True
                feats_load.wait()
            (stage_R0, stage_R1, stage_R2)[i](j)
        elif kind == "W":
            stage_W(i)
        elif kind == "V":
            stage_V(i)
            drain(len(sends) - 60)
        else:
            weight_load.wait()
            turned_weight = weight[...].T
            for b in range(4):
                ig[b * BLOCK : (b + 1) * BLOCK, :] = jnp.dot(
                    csum[b].T, turned_weight, precision=HIGHEST,
                    preferred_element_type=jnp.float32,
                )
            ig_store = load(0, ig, ig_out)

    wg[...] = jnp.concatenate([wgf[: at[EARLY], :], fold(late1)], axis=0).T
    wg_store = load(1, wg, wg_out)
    drain(len(sends))
    ig_store.wait()
    wg_store.wait()


def scratch():
    f32 = jnp.float32
    late = sum(CHUNKS[EARLY:])
    out = [
        pltpu.VMEM((CELLS, BLOCK, BLOCK), f32),
        pltpu.VMEM((CELLS, BLOCK, 2 * BLOCK), jnp.bfloat16),
        pltpu.VMEM((NODE_DEV, WIDTH), f32),
        pltpu.VMEM((NODE_DEV, WIDTH), f32),
        pltpu.VMEM((WIDTH, WIDTH), f32),
        pltpu.VMEM((4, WIDTH, BLOCK), f32),
        pltpu.VMEM((NODE_DEV, WIDTH), f32),
        pltpu.VMEM((WIDTH, WIDTH), f32),
        pltpu.VMEM((WIDTH, WIDTH), f32),
        pltpu.VMEM((late, WIDTH), f32),
        pltpu.VMEM((WIDTH, WIDTH), f32),
        pltpu.VMEM((16, BLOCK), jnp.int32),
        pltpu.SMEM((16, BLOCK), jnp.int32),
        pltpu.VMEM((16, 8, WIDTH), f32),
        pltpu.VMEM((16, 8, WIDTH), f32),
        pltpu.VMEM((16, late, WIDTH), f32),
        pltpu.VMEM((16, late, WIDTH), f32),
        pltpu.SemaphoreType.DMA((5,)),
    ]
    count = 34 * len(CHUNKS) + 80
    out += [pltpu.SemaphoreType.DMA((count,)), pltpu.SemaphoreType.DMA((count,))]
    for j, f in enumerate(CHUNKS):
        landing = (7, 4) if STRAIGHT[j] else (3, 2, 4)
        for lead in (
            (1, 2, 4, 4), (2, 2, 4, 4), (1, 2, 4, 4), (2, 4, 4), landing, (2, 4), (4,),
            (CELLS + 1,),
        ):
            out.append(pltpu.VMEM(lead + (f, BLOCK), f32))
    return out


def local(grad_out, features, weight, adj_values, row_block, col_block, counts):
    anyspace = pl.BlockSpec(memory_space=pl.ANY)
    vmem = pl.BlockSpec(memory_space=pltpu.VMEM)
    return pl.pallas_call(
        kernel,
        out_shape=(
            jax.ShapeDtypeStruct((NODE_DEV, WIDTH), jnp.float32),
            jax.ShapeDtypeStruct((WIDTH, WIDTH), jnp.float32),
        ),
        in_specs=[vmem] * 3 + [anyspace] * 4,
        out_specs=(anyspace, anyspace),
        scratch_shapes=scratch(),
        compiler_params=pltpu.CompilerParams(
            collective_id=0, has_side_effects=True, vmem_limit_bytes=60 * 1024 * 1024
        ),
        cost_estimate=pl.CostEstimate(
            flops=1_200_000_000, bytes_accessed=7_000_000, transcendentals=0
        ),
    )(
        row_block[0].T, col_block[0].T, counts, grad_out, features, weight,
        adj_values.reshape(CELLS, BLOCK, BLOCK),
    )


def solution(mesh):
    return jax.shard_map(
        local,
        mesh=mesh,
        in_specs=(
            P(("col", "row"), None),
            P(("row", "col"), None),
            P(),
            P("col", "row", None, None, None),
            P("col", "row", None),
            P("col", "row", None),
            P("col", "row"),
        ),
        out_specs=(P(("row", "col"), None), P()),
        check_vma=False,
    )
```

time: 426 us -> 94.5 us (0.22)
  waiting for transfers between devices: 366 us -> 0 us
  Pallas kernels: 0 us -> 89.3 us
  matrix products: 26.1 us -> 0 us
  local copies, waits for them, and re-layouts: 18.7 us -> 4.42 us
  between operations: 13.8 us -> 0.64 us
    psum x1 -> x0, waiting for transfers between devices: 244 us -> none  [local(): weight_grad = lax.psum(local_terms, ('row', 'col'))]
    pallas_call x0 -> x1, Pallas kernels: none -> 89.3 us  [local(): pl.pallas_call(kernel, out_shape=(jax.ShapeDtypeStruct((NODE_DEV, WIDTH),...]
    all_gather x1 -> x0, waiting for transfers between devices: 80.7 us -> none  [local(): gathered = lax.all_gather(grad_out, 'row', axis=0, tiled=True)]
    reduce_scatter x1 -> x0, waiting for transfers between devices: 40.6 us -> none  [local(): lax.psum_scatter(partial_value, 'col', scatter_dimension=0, tiled=True)]
    dot_general x4 -> x0, matrix products: 26.1 us -> none  [the longest x1 14.8 us: slot_products(): jnp.einsum('ksab,ksaf->ksbf', part_values, picked, precision=lax.Precisio...]
    dot_general x2 -> x0, local copies, waits for them, and re-layouts: 9.22 us -> none  [the longest x1 6.67 us: slot_products(): jnp.einsum('ksab,ksaf->ksbf', part_values, picked, precision=lax.Precisio...]
    gather x1 -> x0, local copies, waits for them, and re-layouts: 7.03 us -> none  [local(): products = slot_products(values, blocks[block_index])]
  transfers between devices with their start and end apart: 3 -> 0, of which waited for: 3 -> 0; matrix products, arithmetic and copies ran while one was open for 1% -> 0% of each run, Pallas kernels for 0% -> 0%
where the time goes in v2:
time: 94.5 us; the launch traced here: 94.3 us
  Pallas kernels  89.3 us (94%)
  local copies, waits for them, and re-layouts  4.42 us (5%)
    pallas_call x1, Pallas kernels, local(): pl.pallas_call(kernel, out_shape=(jax.ShapeDtypeStruct((NODE_DEV, WIDTH),...  89.3 us
    unnamed x2, local copies, waits for them, and re-layouts  3.14 us

profile of v2, /device:TPU:1, one launch (start us, length us, event | category | flops | bytes accessed | tf_op | source)
XLA Modules:
  0.0 94.3 jit_solution(12417154268491228821)
XLA Ops:
  0.6 1.3 %copy_bitcast_fusion = (s32[3,32]{1,0:T(4,128)}, s32[3,32]{1,0:T(4,128)}) fusion(s32[1,32,3]{1,0,2:T(1,128)} %param.12, s32[1,32,3]{1,0,2:T(1,128)} %param.11), kind=kLoop, calls=%fused_computation | loop fusion | bytes 1536 | tf_op jit(solution)/shard_map/transpose | solution.py:454
  1.9 89.3 %shard_map.86 = (f32[512,128]{1,0:T(8,128)}, f32[128,128]{1,0:T(8,128)}) custom-call(s32[3,32]{1,0:T(4,128)} %get-tuple-element.3.rowb, s32[3,32]{1,0:T(4,128)} %get-tuple-element.2.colb, s32[1,32]{1,0:T(1,128)} %counts.1, f32[512,128]{1,0:T(8,128)} %grad_hbm.1, f32[512,128]{1,0:T(8,128)} %feats_hbm.1, f32[128,128]{1,0:T(8,128)} %weight_hbm.1, ...), custom_call_target="tpu_custom_call" | custom-call | flops 1200000000 | bytes 7000000 | tf_op jit(solution)/shard_map/pallas_call | solution.py:438
  91.2 1.7 %copy.15 = f32[512,128]{1,0:T(8,128)} copy(f32[512,128]{1,0:T(8,128)} %get-tuple-element.6) | data formatting | bytes 524288
  92.9 1.5 %copy.16 = f32[128,128]{1,0:T(8,128)} copy(f32[128,128]{1,0:T(8,128)} %get-tuple-element.7) | data formatting | bytes 131072

commit v3 on v2

--- a/solution.py
+++ b/solution.py
@@ -14,18 +14,18 @@
 PARTS = ((0, 0, 24), (1, 24, 24), (1, 48, 24), (2, 72, 24))
 COL_BLOCKS = 32
 NODE_DEV = 512
-CHUNKS = (16, 32, 32, 32, 16)
-ACROSS = (1, 1, 1, 0, 0)
-STRAIGHT = (0, 0, 0, 0, 1)
-EARLY = 4
+CHUNKS = (24, 40, 40, 24)
+ACROSS = (0, 0, 1, 1)
+ROUTES = ('y', 'y', 'y', 'z')
+EARLY = 3
 ORDER = (
-    ("U0", 0), ("U0", 1), ("U0", 2), ("U1", 0), ("U1", 1), ("U1", 2), ("U2", 0), ("C0", 0), ("U0", 3), ("U2", 1),
-    ("C0", 1), ("U2", 2), ("U3", 0), ("C0", 2), ("U0", 4), ("C1", 0), ("C2", 0), ("U1", 3), ("U3", 1), ("U3", 2),
-    ("U4", 0), ("C1", 1), ("C2", 1), ("U1", 4), ("C1", 2), ("C3", 0), ("R0", 0), ("U2", 3), ("U4", 1), ("C2", 2),
-    ("U4", 2), ("C0", 3), ("C3", 1), ("U2", 4), ("R0", 1), ("C3", 2), ("R0", 2), ("C0", 4), ("U3", 3), ("R1", 0),
-    ("U3", 4), ("C1", 3), ("C2", 3), ("U4", 3), ("C1", 4), ("R2", 0), ("U4", 4), ("C2", 4), ("C3", 3), ("R0", 3),
-    ("C3", 4), ("R0", 4), ("R1", 1), ("R1", 2), ("R2", 1), ("R2", 2), ("R1", 3), ("R2", 4), ("W0", 0), ("R2", 3),
-    ("V0", 0), ("O0", 0), ("W1", 0), ("V1", 0), ("W2", 0), ("V2", 0), ("V3", 0),
+    ("U0", 0), ("U0", 1), ("F0", 0), ("U1", 0), ("U1", 1), ("F1", 0), ("F2", 0), ("U0", 2), ("U2", 0), ("U0", 3),
+    ("C0", 0), ("U2", 1), ("C0", 1), ("F3", 0), ("U3", 0), ("U1", 2), ("C1", 0), ("C2", 0), ("U1", 3), ("U3", 1),
+    ("U4", 0), ("F4", 0), ("C1", 1), ("C3", 0), ("R0", 0), ("U2", 2), ("G0", 0), ("C2", 1), ("C0", 2), ("U2", 3),
+    ("U4", 1), ("C0", 3), ("C3", 1), ("R0", 1), ("U3", 2), ("G0", 1), ("R1", 0), ("U3", 3), ("C1", 2), ("C2", 2),
+    ("U4", 2), ("C1", 3), ("C2", 3), ("R2", 0), ("C3", 2), ("U4", 3), ("R0", 2), ("G0", 2), ("V0", 0), ("C3", 3),
+    ("R0", 3), ("G0", 3), ("W0", 0), ("R1", 1), ("V1", 0), ("R1", 3), ("R1", 2), ("R2", 1), ("V2", 0), ("W1", 0),
+    ("R2", 3), ("R2", 2), ("O0", 0), ("V3", 0), ("W2", 0),
 )
 MESH = pl.DeviceIdType.MESH
 HIGHEST = lax.Precision.HIGHEST
@@ -50,7 +50,7 @@
     spare = jnp.zeros((1, SECTIONS), jnp.int32)
 
     def flat(ref):
-        return jnp.concatenate([ref[0:1, :], ref[1:2, :], ref[2:3, :], spare], axis=1)
+        return jnp.concatenate([ref[0], ref[1], ref[2], spare], axis=1)
 
     rb, cb = flat(rowb), flat(colb)
     live = s < jnp.concatenate([counts[0:1, :]] * 4, axis=1)
@@ -84,7 +84,7 @@
 
 def kernel(
     rowb, colb, counts, grad_hbm, feats_hbm, weight_hbm, adj_hbm, ig_out, wg_out,
-    adj, halves, grad, feats, weight, csum, ig, wg, wgt, wgl, wgf, ordered, meta,
+    adj, halves, grad, feats, fhalves, weight, csum, wgt, wgl, wgf, ordered, meta,
     tiles, crossed, late0, late1, local_sem, send_sem, recv_sem, *bufs,
 ):
     n = len(CHUNKS)
@@ -125,7 +125,7 @@
 
     grad_load = load(0, grad_hbm, grad)
     adj_load = load(1, adj_hbm, adj)
-    feats_load = load(2, feats_hbm, feats)
+    feats_load = load(2, feats_hbm, feats.at[0, 0])
     weight_load = load(3, weight_hbm, weight)
 
     barrier = pltpu.get_barrier_semaphore()
@@ -236,7 +236,7 @@
             run[p] = acc
             return acc
 
-        lax.fori_loop(begin, begin + size, step, init, unroll=4)
+        lax.fori_loop(begin, begin + size, step, init, unroll=24)
 
     def collect(j):
         part_sums, run = chunk_bufs[j][3], chunk_bufs[j][7]
@@ -247,14 +247,16 @@
             part_sums[m // 16, (m // 4) % 4, m % 4] = (v[0] + v[1]) + v[2]
             return carry
 
-        lax.fori_loop(0, COL_BLOCKS, body, 0, unroll=4)
+        lax.fori_loop(0, COL_BLOCKS, body, 0, unroll=8)
 
     def stage_R0(j):
         collect(j)
-        p, landing = chunk_bufs[j][3:5]
-        if STRAIGHT[j]:
+        p, landing, s, second = chunk_bufs[j][3:7]
+        if ROUTES[j] == "direct":
             for i, (a, b) in enumerate(col_steps):
                 push(("R0", j), p.at[a, b], landing.at[i], col_peers[a, b])
+        elif ROUTES[j] == "z":
+            push(("R0", j), p.at[1], second, col_peers[1, 0])
         else:
             for d in range(1, 4):
                 push(("R0", j), p.at[:, d], landing.at[d - 1], col_peers[0, d])
@@ -262,27 +264,75 @@
     def stage_R1(j):
         p, landing, s, second = chunk_bufs[j][3:7]
         take("R0", j)
-        for z in range(2):
-            s[z] = (p[z, 0] + landing[0, z]) + (landing[1, z] + landing[2, z])
-        push(("R1", j), s.at[1], second, col_peers[1, 0])
+        if ROUTES[j] == "z":
+            for d in (1, 2, 3, 0):
+                s[d] = p[0, d] + second[d]
+                if d:
+                    push(("R1", j), s.at[d], landing.at[d - 1], col_peers[0, d])
+        else:
+            for z in (1, 0):
+                s[z] = (p[z, 0] + landing[0, z]) + (landing[1, z] + landing[2, z])
+                if z:
+                    push(("R1", j), s.at[1], second, col_peers[1, 0])
 
     def stage_R2(j):
         p, landing, s, second = chunk_bufs[j][3:7]
-        f = CHUNKS[j]
-        take("R0" if STRAIGHT[j] else "R1", j)
-        total = jnp.zeros((f, WIDTH), jnp.float32)
+        take("R0" if ROUTES[j] == "direct" else "R1", j)
         for b in range(4):
-            if STRAIGHT[j]:
+            if ROUTES[j] == "direct":
                 v = p[0, 0, b]
                 for i in range(7):
                     v += landing[i, b]
+            elif ROUTES[j] == "z":
+                v = (s[0, b] + landing[0, b]) + (landing[1, b] + landing[2, b])
             else:
                 v = s[0, b] + second[b]
-            csum[b, at[j] : at[j] + f, :] = v
-            total += jnp.dot(
-                v, feats[b * BLOCK : (b + 1) * BLOCK, :], precision=HIGHEST,
-                preferred_element_type=jnp.float32,
-            )
+            csum[b, at[j] : at[j] + CHUNKS[j], :] = v
+
+    def stage_F(i):
+        first, rest = pl.ds(0, 2), pl.ds(2, 2)
+        if i == 0:
+            feats_load.wait()
+            own = feats.at[0, 0]
+            push(("F0",), own, feats.at[0, 3], col_peers[0, 1])
+            push(("F0",), own, feats.at[0, 1], col_peers[0, 3])
+            push(("Fz",), own, feats.at[1, 0], col_peers[1, 0])
+        elif i == 1:
+            take("Fz")
+            push(("F1",), feats.at[1, 0], feats.at[1, 3], col_peers[0, 1])
+            push(("F1",), feats.at[1, 0], feats.at[1, 1], col_peers[0, 3])
+        elif i == 2:
+            take("F0")
+            push(("F2",), feats.at[0, 3, first], feats.at[0, 2, first], col_peers[0, 1])
+            push(("F2",), feats.at[0, 1, rest], feats.at[0, 2, rest], col_peers[0, 3])
+        elif i == 3:
+            take("F1")
+            push(("F3",), feats.at[1, 3, first], feats.at[1, 2, first], col_peers[0, 1])
+            push(("F3",), feats.at[1, 1, rest], feats.at[1, 2, rest], col_peers[0, 3])
+        else:
+            take("F2")
+            take("F3")
+
+            def body(m, carry):
+                high, low = split(feats[m // 16, (m // 4) % 4, m % 4])
+                fhalves[m, :, :BLOCK] = high.astype(jnp.bfloat16)
+                fhalves[m, :, BLOCK:] = low.astype(jnp.bfloat16)
+                return carry
+
+            lax.fori_loop(0, COL_BLOCKS, body, 0, unroll=2)
+
+    def stage_G(j):
+        f, p = CHUNKS[j], chunk_bufs[j][3]
+
+        def body(m, total):
+            high, low = split(p[m // 16, (m // 4) % 4, m % 4])
+            both = jnp.concatenate([high, low], axis=0).astype(jnp.bfloat16)
+            return total + jnp.dot(both, fhalves[m], preferred_element_type=jnp.float32)
+
+        r = lax.fori_loop(
+            0, COL_BLOCKS, body, jnp.zeros((2 * f, 2 * BLOCK), jnp.float32), unroll=8
+        )
+        total = r[:f, :BLOCK] + (r[f:, :BLOCK] + r[:f, BLOCK:])
         if j < EARLY:
             wgt[at[j] : at[j] + f, :] = total
         else:
@@ -301,36 +351,36 @@
         if i == 0:
             wgt[at[EARLY] :, :] = jnp.zeros((WIDTH - at[EARLY], WIDTH), jnp.float32)
             for d in range(1, 16):
-                to = (pillar + d) % 16
-                push(("V0",), tile(wgt, to), tiles.at[pillar], pillar_peers[d - 1])
-            tiles[pillar] = wgt[pl.ds(pl.multiple_of(pillar * 8, 8), 8), :]
+                to = (deck + d) % 16
+                push(("V0",), tile(wgt, to), tiles.at[deck], deck_peers[d - 1])
+            tiles[deck] = wgt[pl.ds(pl.multiple_of(deck * 8, 8), 8), :]
         elif i == 1:
             take("V0")
-            crossed[deck] = fold(tiles)
+            crossed[pillar] = fold(tiles)
             for d in range(1, 16):
-                push(("V1",), crossed.at[deck], crossed.at[deck], deck_peers[d - 1])
+                push(("V1",), crossed.at[pillar], crossed.at[pillar], pillar_peers[d - 1])
         elif i == 2:
             take("V1")
-            wgf[pl.ds(pl.multiple_of(pillar * 8, 8), 8), :] = fold(crossed)
+            wgf[pl.ds(pl.multiple_of(deck * 8, 8), 8), :] = fold(crossed)
             for d in range(1, 16):
-                push(("V2",), tile(wgf, pillar), tile(wgf, pillar), pillar_peers[d - 1])
+                push(("V2",), tile(wgf, deck), tile(wgf, deck), deck_peers[d - 1])
         else:
             take("V2")
 
     def stage_W(i):
         if i == 0:
-            late0[pillar] = wgl[...]
+            late0[deck] = wgl[...]
             for d in range(1, 16):
-                push(("W0",), late0.at[pillar], late0.at[pillar], pillar_peers[d - 1])
+                push(("W0",), late0.at[deck], late0.at[deck], deck_peers[d - 1])
         elif i == 1:
             take("W0")
-            late1[deck] = fold(late0)
+            late1[pillar] = fold(late0)
             for d in range(1, 16):
-                push(("W1",), late1.at[deck], late1.at[deck], deck_peers[d - 1])
+                push(("W1",), late1.at[pillar], late1.at[pillar], pillar_peers[d - 1])
         else:
             take("W1")
 
-    parts, state = 8, {"done": 0, "sent": 0, "feats": False}
+    parts, state = 8, {"done": 0, "sent": 0}
 
     def prepare():
         i = state["done"]
@@ -353,7 +403,7 @@
                 halves[s, :, BLOCK:] = low.astype(jnp.bfloat16)
                 return carry
 
-            lax.fori_loop((i - 1) * size, i * size, body, 0, unroll=2)
+            lax.fori_loop((i - 1) * size, i * size, body, 0, unroll=4)
 
     def drain(upto):
         while state["sent"] < upto:
@@ -371,12 +421,13 @@
         elif kind == "C":
             stage_C(j, i)
         elif kind == "R":
-            if name == "R2" and not state["feats"]:
-                state["feats"] = True
-                feats_load.wait()
             (stage_R0, stage_R1, stage_R2)[i](j)
         elif kind == "W":
             stage_W(i)
+        elif kind == "F":
+            stage_F(i)
+        elif kind == "G":
+            stage_G(j)
         elif kind == "V":
             stage_V(i)
             drain(len(sends) - 60)
@@ -384,17 +435,13 @@
             weight_load.wait()
             turned_weight = weight[...].T
             for b in range(4):
-                ig[b * BLOCK : (b + 1) * BLOCK, :] = jnp.dot(
+                ig_out[b * BLOCK : (b + 1) * BLOCK, :] = jnp.dot(
                     csum[b].T, turned_weight, precision=HIGHEST,
                     preferred_element_type=jnp.float32,
                 )
-            ig_store = load(0, ig, ig_out)
-
-    wg[...] = jnp.concatenate([wgf[: at[EARLY], :], fold(late1)], axis=0).T
-    wg_store = load(1, wg, wg_out)
+
+    wg_out[...] = jnp.concatenate([wgf[: at[EARLY], :], fold(late1)], axis=0).T
     drain(len(sends))
-    ig_store.wait()
-    wg_store.wait()
 
 
 def scratch():
@@ -404,11 +451,10 @@
         pltpu.VMEM((CELLS, BLOCK, BLOCK), f32),
         pltpu.VMEM((CELLS, BLOCK, 2 * BLOCK), jnp.bfloat16),
         pltpu.VMEM((NODE_DEV, WIDTH), f32),
-        pltpu.VMEM((NODE_DEV, WIDTH), f32),
+        pltpu.VMEM((2, 4, 4, BLOCK, WIDTH), f32),
+        pltpu.VMEM((COL_BLOCKS, BLOCK, 2 * WIDTH), jnp.bfloat16),
         pltpu.VMEM((WIDTH, WIDTH), f32),
         pltpu.VMEM((4, WIDTH, BLOCK), f32),
-        pltpu.VMEM((NODE_DEV, WIDTH), f32),
-        pltpu.VMEM((WIDTH, WIDTH), f32),
         pltpu.VMEM((WIDTH, WIDTH), f32),
         pltpu.VMEM((late, WIDTH), f32),
         pltpu.VMEM((WIDTH, WIDTH), f32),
@@ -420,12 +466,16 @@
         pltpu.VMEM((16, late, WIDTH), f32),
         pltpu.SemaphoreType.DMA((5,)),
     ]
-    count = 34 * len(CHUNKS) + 80
+    count = 34 * len(CHUNKS) + 90
     out += [pltpu.SemaphoreType.DMA((count,)), pltpu.SemaphoreType.DMA((count,))]
     for j, f in enumerate(CHUNKS):
-        landing = (7, 4) if STRAIGHT[j] else (3, 2, 4)
+        landing, summed, second = {
+            "direct": ((7, 4), (1,), (1,)),
+            "z": ((3, 4), (4, 4), (4, 4)),
+            "y": ((3, 2, 4), (2, 4), (4,)),
+        }[ROUTES[j]]
         for lead in (
-            (1, 2, 4, 4), (2, 2, 4, 4), (1, 2, 4, 4), (2, 4, 4), landing, (2, 4), (4,),
+            (1, 2, 4, 4), (2, 2, 4, 4), (1, 2, 4, 4), (2, 4, 4), landing, summed, second,
             (CELLS + 1,),
         ):
             out.append(pltpu.VMEM(lead + (f, BLOCK), f32))
@@ -433,7 +483,7 @@
 
 
 def local(grad_out, features, weight, adj_values, row_block, col_block, counts):
-    anyspace = pl.BlockSpec(memory_space=pl.ANY)
+    hbm = pl.BlockSpec(memory_space=pltpu.HBM)
     vmem = pl.BlockSpec(memory_space=pltpu.VMEM)
     return pl.pallas_call(
         kernel,
@@ -441,8 +491,8 @@
             jax.ShapeDtypeStruct((NODE_DEV, WIDTH), jnp.float32),
             jax.ShapeDtypeStruct((WIDTH, WIDTH), jnp.float32),
         ),
-        in_specs=[vmem] * 3 + [anyspace] * 4,
-        out_specs=(anyspace, anyspace),
+        in_specs=[vmem] * 3 + [hbm] * 4,
+        out_specs=(vmem, vmem),
         scratch_shapes=scratch(),
         compiler_params=pltpu.CompilerParams(
             collective_id=0, has_side_effects=True, vmem_limit_bytes=60 * 1024 * 1024
@@ -451,7 +501,8 @@
             flops=1_200_000_000, bytes_accessed=7_000_000, transcendentals=0
         ),
     )(
-        row_block[0].T, col_block[0].T, counts, grad_out, features, weight,
+        row_block.transpose(2, 0, 1), col_block.transpose(2, 0, 1), counts, grad_out,
+        features.reshape(4, BLOCK, WIDTH), weight,
         adj_values.reshape(CELLS, BLOCK, BLOCK),
     )
 

time: 94.5 us -> 82 us (0.87)
  Pallas kernels: 89.3 us -> 78 us
  local copies, waits for them, and re-layouts: 4.42 us -> 3.14 us
    pallas_call x1, Pallas kernels: 89.3 us -> 78 us  [local(): pl.pallas_call(kernel, out_shape=(jax.ShapeDtypeStruct((NODE_DEV, WIDTH),...]
    transpose x1 -> x0, local copies, waits for them, and re-layouts: 1.28 us -> none  [local(): col_block[0]]
where the time goes in v3:
time: 82 us; the launch traced here: 81.8 us
  Pallas kernels  78 us (95%)
  local copies, waits for them, and re-layouts  3.14 us (4%)
    pallas_call x1, Pallas kernels, local(): pl.pallas_call(kernel, out_shape=(jax.ShapeDtypeStruct((NODE_DEV, WIDTH),...  78 us
    unnamed x2, local copies, waits for them, and re-layouts  3.14 us

profile of v3, /device:TPU:1, one launch (start us, length us, event | category | flops | bytes accessed | tf_op | source)
XLA Modules:
  0.0 81.8 jit_solution(4245231864365777666)
XLA Ops:
  0.6 78.0 %shard_map.86 = (f32[512,128]{1,0:T(8,128)}, f32[128,128]{1,0:T(8,128)}) custom-call(s32[3,1,32]{2,1,0:T(1,128)} %bitcast.6, s32[3,1,32]{2,1,0:T(1,128)} %bitcast.7, s32[1,32]{1,0:T(1,128)} %counts.1, f32[512,128]{1,0:T(8,128)} %grad_hbm.1, f32[4,128,128]{2,1,0:T(8,128)} %bitcast.5, f32[128,128]{1,0:T(8,128)} %weight_hbm.1, f32[96,128,128]{2,1,0:T(8,128)} %bitcast.4), custom_call_target="tpu_custom_call" | custom-call | flops 1200000000 | bytes 7000000 | tf_op jit(solution)/shard_map/pallas_call | solution.py:488
  78.6 1.7 %copy.11 = f32[512,128]{1,0:T(8,128)} copy(f32[512,128]{1,0:T(8,128)} %get-tuple-element.4) | data formatting | bytes 524288
  80.3 1.5 %copy.12 = f32[128,128]{1,0:T(8,128)} copy(f32[128,128]{1,0:T(8,128)} %get-tuple-element.5) | data formatting | bytes 131072

commit v4 on v3

--- a/solution.py
+++ b/solution.py
@@ -19,13 +19,13 @@
 ROUTES = ('y', 'y', 'y', 'z')
 EARLY = 3
 ORDER = (
-    ("U0", 0), ("U0", 1), ("F0", 0), ("U1", 0), ("U1", 1), ("F1", 0), ("F2", 0), ("U0", 2), ("U2", 0), ("U0", 3),
-    ("C0", 0), ("U2", 1), ("C0", 1), ("F3", 0), ("U3", 0), ("U1", 2), ("C1", 0), ("C2", 0), ("U1", 3), ("U3", 1),
-    ("U4", 0), ("F4", 0), ("C1", 1), ("C3", 0), ("R0", 0), ("U2", 2), ("G0", 0), ("C2", 1), ("C0", 2), ("U2", 3),
-    ("U4", 1), ("C0", 3), ("C3", 1), ("R0", 1), ("U3", 2), ("G0", 1), ("R1", 0), ("U3", 3), ("C1", 2), ("C2", 2),
-    ("U4", 2), ("C1", 3), ("C2", 3), ("R2", 0), ("C3", 2), ("U4", 3), ("R0", 2), ("G0", 2), ("V0", 0), ("C3", 3),
-    ("R0", 3), ("G0", 3), ("W0", 0), ("R1", 1), ("V1", 0), ("R1", 3), ("R1", 2), ("R2", 1), ("V2", 0), ("W1", 0),
-    ("R2", 3), ("R2", 2), ("O0", 0), ("V3", 0), ("W2", 0),
+    ("U0", 0), ("U0", 1), ("F0", 0), ("U1", 0), ("U1", 1), ("F1", 0), ("F2", 0), ("U0", 2), ("U2", 0), ("U0",
+    3), ("C0", 0), ("U2", 1), ("C0", 1), ("F3", 0), ("U3", 0), ("U1", 2), ("C1", 0), ("C2", 0), ("U1", 3),
+    ("U3", 1), ("U4", 0), ("F4", 0), ("C1", 1), ("C3", 0), ("R0", 0), ("U2", 2), ("G0", 0), ("C2", 1), ("C0",
+    2), ("U2", 3), ("U4", 1), ("C0", 3), ("C3", 1), ("R0", 1), ("U3", 2), ("G0", 1), ("R1", 0), ("U3", 3),
+    ("C1", 2), ("C2", 2), ("U4", 2), ("C1", 3), ("C2", 3), ("R2", 0), ("C3", 2), ("U4", 3), ("R0", 2), ("G0",
+    2), ("V0", 0), ("C3", 3), ("R0", 3), ("G0", 3), ("W0", 0), ("R1", 1), ("V1", 0), ("R1", 3), ("R1", 2),
+    ("R2", 1), ("W1", 0), ("V2", 0), ("R2", 3), ("R2", 2), ("O0", 0), ("W2", 0), ("V3", 0),
 )
 MESH = pl.DeviceIdType.MESH
 HIGHEST = lax.Precision.HIGHEST
@@ -84,7 +84,7 @@
 
 def kernel(
     rowb, colb, counts, grad_hbm, feats_hbm, weight_hbm, adj_hbm, ig_out, wg_out,
-    adj, halves, grad, feats, fhalves, weight, csum, wgt, wgl, wgf, ordered, meta,
+    adj, halves, grad, feats, fhalves, weight, csum, ig, wgt, wgl, wgf, ordered, meta,
     tiles, crossed, late0, late1, local_sem, send_sem, recv_sem, *bufs,
 ):
     n = len(CHUNKS)
@@ -430,18 +430,21 @@
             stage_G(j)
         elif kind == "V":
             stage_V(i)
-            drain(len(sends) - 60)
+            if i:
+                drain(len(sends) - 60 if i < 3 else len(sends) - 15)
         else:
             weight_load.wait()
             turned_weight = weight[...].T
             for b in range(4):
-                ig_out[b * BLOCK : (b + 1) * BLOCK, :] = jnp.dot(
+                ig[b * BLOCK : (b + 1) * BLOCK, :] = jnp.dot(
                     csum[b].T, turned_weight, precision=HIGHEST,
                     preferred_element_type=jnp.float32,
                 )
+            ig_store = load(0, ig, ig_out)
 
     wg_out[...] = jnp.concatenate([wgf[: at[EARLY], :], fold(late1)], axis=0).T
     drain(len(sends))
+    ig_store.wait()
 
 
 def scratch():
@@ -455,6 +458,7 @@
         pltpu.VMEM((COL_BLOCKS, BLOCK, 2 * WIDTH), jnp.bfloat16),
         pltpu.VMEM((WIDTH, WIDTH), f32),
         pltpu.VMEM((4, WIDTH, BLOCK), f32),
+        pltpu.VMEM((NODE_DEV, WIDTH), f32),
         pltpu.VMEM((WIDTH, WIDTH), f32),
         pltpu.VMEM((late, WIDTH), f32),
         pltpu.VMEM((WIDTH, WIDTH), f32),
@@ -492,7 +496,7 @@
             jax.ShapeDtypeStruct((WIDTH, WIDTH), jnp.float32),
         ),
         in_specs=[vmem] * 3 + [hbm] * 4,
-        out_specs=(vmem, vmem),
+        out_specs=(pl.BlockSpec(memory_space=pl.ANY), vmem),
         scratch_shapes=scratch(),
         compiler_params=pltpu.CompilerParams(
             collective_id=0, has_side_effects=True, vmem_limit_bytes=60 * 1024 * 1024

time: 82 us -> 82 us (level)
  no operation moved by 1% of the time
where the time goes in v4:
time: 82 us; the launch traced here: 81.8 us
  Pallas kernels  78 us (95%)
  local copies, waits for them, and re-layouts  3.14 us (4%)
    pallas_call x1, Pallas kernels, local(): pl.pallas_call(kernel, out_shape=(jax.ShapeDtypeStruct((NODE_DEV, WIDTH),...  78 us
    unnamed x2, local copies, waits for them, and re-layouts  3.14 us

profile of v4, /device:TPU:1, one launch (start us, length us, event | category | flops | bytes accessed | tf_op | source)
XLA Modules:
  0.0 81.8 jit_solution(3985861881143777572)
XLA Ops:
  0.6 78.0 %shard_map.86 = (f32[512,128]{1,0:T(8,128)}, f32[128,128]{1,0:T(8,128)}) custom-call(s32[3,1,32]{2,1,0:T(1,128)} %bitcast.6, s32[3,1,32]{2,1,0:T(1,128)} %bitcast.7, s32[1,32]{1,0:T(1,128)} %counts.1, f32[512,128]{1,0:T(8,128)} %grad_hbm.1, f32[4,128,128]{2,1,0:T(8,128)} %bitcast.5, f32[128,128]{1,0:T(8,128)} %weight_hbm.1, f32[96,128,128]{2,1,0:T(8,128)} %bitcast.4), custom_call_target="tpu_custom_call" | custom-call | flops 1200000000 | bytes 7000000 | tf_op jit(solution)/shard_map/pallas_call | solution.py:492
  78.6 1.7 %copy.11 = f32[512,128]{1,0:T(8,128)} copy(f32[512,128]{1,0:T(8,128)} %get-tuple-element.4) | data formatting | bytes 524288
  80.3 1.5 %copy.12 = f32[128,128]{1,0:T(8,128)} copy(f32[128,128]{1,0:T(8,128)} %get-tuple-element.5) | data formatting | bytes 131072
